TPU v7x, 256 devices: a whole 4x4x8 slice. The times are simulated.
256 devices in a mesh: dp: 16 (over x, z_lo, core), seq: 16 (over y, z_hi).
Axes of the slice: x: 4, y: 4, z: 8 (z_hi: 4, z_lo: 2; z = z_hi * 2 + z_lo), core: 2. Of those that a mesh axis runs over, the one named last changes fastest.
Arguments:
- query_in: bfloat16 [512, 262144], P('dp', 'seq'), may hold values from -6 to 6
- key_in: bfloat16 [512, 262144], P('dp', 'seq'), may hold values from -6 to 6
- values_in: bfloat16 [512, 262144], P('dp', 'seq'), may hold values from -6 to 6
- kernel: bfloat16 [512, 262144], P('dp', 'seq'), may hold values from -6 to 6
- cotangent: bfloat16 [512, 262144], P('dp', 'seq'), may hold values from -6 to 6
- right_in: bfloat16 [512, 512], P('dp'), may hold values from -0.25 to 0.25
- left_in: bfloat16 [512, 512], P('dp'), may hold values from -0.25 to 0.25
- right_out: bfloat16 [512, 512], P('dp'), may hold values from -0.25 to 0.25
- left_out: bfloat16 [512, 512], P('dp'), may hold values from -0.25 to 0.25
- twiddle_one: float32 [512, 512], P(None, 'seq'), may hold values from 0.5 to 2
- twiddle_two: float32 [512, 512], P(None, 'seq'), may hold values from 0.5 to 2
Outputs:
- mixed_out: bfloat16 [512, 262144], P('dp', 'seq')
- grad_query: bfloat16 [512, 262144], P('dp', 'seq')
- grad_key: bfloat16 [512, 262144], P('dp', 'seq')
- grad_value: bfloat16 [512, 262144], P('dp', 'seq')
- grad_kernel: bfloat16 [512, 262144], P('dp', 'seq')
- grad_right_in: float32 [512, 512], P('dp')
- grad_left_in: float32 [512, 512], P('dp')
- grad_right_out: float32 [512, 512], P('dp')
- grad_left_out: float32 [512, 512], P('dp')
All inputs are finite; a program needn't handle non-finite values.
Results may differ from a plain program's by a relative error of at most 0.03.
Values may be sent and summed in bfloat16 or wider, within the bound.
A program may use at most 128 MiB of HBM per device.

v0:
```python
import math

import jax
import jax.numpy as jnp
from jax import lax
from jax.sharding import PartitionSpec as P

C = 512
NB = 512
BS = 512


def term_maker(first, second, form, scale):

    def term(start, count):
        return jnp.einsum(form, first, second, preferred_element_type=jnp.float32) * scale

    return term


def reduce_factor(term, total_rows):
    owned = lax.psum_scatter(
        term(jnp.int32(0), total_rows // lax.axis_size("dp") * lax.axis_size("dp")).astype(
            jnp.bfloat16
        ),
        "dp",
        scatter_dimension=0,
        tiled=True,
    )
    return lax.psum(owned, "seq").astype(jnp.float32)


def shards(
    query_in,
    key_in,
    values_in,
    kernel,
    cotangent,
    right_in,
    left_in,
    right_out,
    left_out,
    twiddle_one,
    twiddle_two,
):
    scale = 1.0 / math.sqrt(C * NB)
    chans = query_in.shape[0]
    blocks_own = query_in.shape[1] // BS
    inner_own = kernel.shape[1] // NB
    query = query_in.reshape(chans, blocks_own, BS)
    key = key_in.reshape(chans, blocks_own, BS)
    values = values_in.reshape(chans, blocks_own, BS)
    grad_out = cotangent.reshape(chans, blocks_own, BS)
    kern = kernel.reshape(chans, inner_own, NB)
    full_rin, full_lin, full_rout, full_lout = (
        lax.all_gather(right_in, "dp", axis=0, tiled=True),
        lax.all_gather(left_in, "dp", axis=0, tiled=True),
        lax.all_gather(right_out, "dp", axis=0, tiled=True),
        lax.all_gather(left_out, "dp", axis=0, tiled=True),
    )
    paired = (key.astype(jnp.float32) * values.astype(jnp.float32)).astype(jnp.bfloat16)
    spread = jnp.einsum("cij,jk->cki", paired, full_rin, preferred_element_type=jnp.float32)
    twisted = (spread * twiddle_one[None]).astype(jnp.bfloat16)
    exchanged = lax.all_to_all(twisted, "seq", split_axis=1, concat_axis=2, tiled=True)
    turned = exchanged
    mixed_one = jnp.einsum("cji,ik->cjk", exchanged, full_lin, preferred_element_type=jnp.float32)
    weighted = (mixed_one * kern.astype(jnp.float32)).astype(jnp.bfloat16)
    spread_two = jnp.einsum("cji,ik->ckj", weighted, full_rout, preferred_element_type=jnp.float32)
    twisted_two = (spread_two * twiddle_two[None]).astype(jnp.bfloat16)
    exchanged = lax.all_to_all(twisted_two, "seq", split_axis=1, concat_axis=2, tiled=True)
    mixed_two = jnp.einsum("cij,jk->cik", exchanged, full_lout, preferred_element_type=jnp.float32)
    mixed_out = (query.astype(jnp.float32) * mixed_two).astype(jnp.bfloat16)
    grads = {}

    def settle(name, term, total_rows):
        grads[name] = reduce_factor(term, total_rows)

    grad_query = (grad_out.astype(jnp.float32) * mixed_two).astype(jnp.bfloat16)
    grad_mixed = (grad_out.astype(jnp.float32) * query.astype(jnp.float32)).astype(jnp.bfloat16)
    settle("left_out", term_maker(exchanged, grad_mixed, "cij,cik->jk", scale), exchanged.shape[2])
    back_two = jnp.einsum(
        "cik,jk->cji", grad_mixed, full_lout, preferred_element_type=jnp.float32
    ).astype(jnp.bfloat16)
    grad_twisted = (
        lax.all_to_all(back_two, "seq", split_axis=1, concat_axis=2, tiled=True).astype(jnp.float32)
        * jnp.transpose(twiddle_two)[None]
    ).astype(jnp.bfloat16)
    settle("right_out", term_maker(weighted, grad_twisted, "cji,cjk->ik", scale), weighted.shape[2])
    grad_weighted = jnp.einsum(
        "cjk,ik->cji", grad_twisted, full_rout, preferred_element_type=jnp.float32
    )
    grad_kernel = (grad_weighted * mixed_one).astype(jnp.bfloat16)
    grad_mixed_one = (grad_weighted * kern.astype(jnp.float32)).astype(jnp.bfloat16)
    settle("left_in", term_maker(turned, grad_mixed_one, "cji,cjk->ik", scale), turned.shape[2])
    back_one = jnp.einsum(
        "cjk,ik->cij", grad_mixed_one, full_lin, preferred_element_type=jnp.float32
    ).astype(jnp.bfloat16)
    grad_spread = (
        lax.all_to_all(back_one, "seq", split_axis=1, concat_axis=2, tiled=True).astype(jnp.float32)
        * jnp.transpose(twiddle_one)[None]
    ).astype(jnp.bfloat16)
    settle("right_in", term_maker(paired, grad_spread, "cij,cik->jk", scale), paired.shape[2])
    grad_paired = jnp.einsum(
        "cik,jk->cij", grad_spread, full_rin, preferred_element_type=jnp.float32
    )
    grad_key = (grad_paired * values.astype(jnp.float32)).astype(jnp.bfloat16)
    grad_value = (grad_paired * key.astype(jnp.float32)).astype(jnp.bfloat16)
    flat = chans * blocks_own * BS
    return (
        mixed_out.reshape(chans, flat // chans),
        grad_query.reshape(chans, flat // chans),
        grad_key.reshape(chans, flat // chans),
        grad_value.reshape(chans, flat // chans),
        grad_kernel.reshape(chans, flat // chans),
        grads["right_in"],
        grads["left_in"],
        grads["right_out"],
        grads["left_out"],
    )


def solution(mesh):
    in_specs = (
        P("dp", "seq"),
        P("dp", "seq"),
        P("dp", "seq"),
        P("dp", "seq"),
        P("dp", "seq"),
        P("dp", None),
        P("dp", None),
        P("dp", None),
        P("dp", None),
        P(None, "seq"),
        P(None, "seq"),
    )
    out_specs = (
        P("dp", "seq"),
        P("dp", "seq"),
        P("dp", "seq"),
        P("dp", "seq"),
        P("dp", "seq"),
        P("dp", None),
        P("dp", None),
        P("dp", None),
        P("dp", None),
    )
    return jax.shard_map(shards, mesh=mesh, in_specs=in_specs, out_specs=out_specs, check_vma=False)
```

profile of v0, /device:TPU:2, one launch (start us, length us, event | category | flops | bytes accessed | tf_op | source)
XLA Modules:
  0.0 688.0 jit_solution(11803542544663233207)
XLA Ops:
  9.6 19.7 %all_gather.12 = bf16[512,512]{1,0:T(8,128)(2,1)S(1)} all-gather(bf16[32,512]{1,0:T(8,128)(2,1)S(1)} %copy-done.17), channel_id=1, replica_groups=mesh['dp'=16,'seq'=16] {'dp'}, dimensions={0}, use_global_device_ids=true | all-gather | bytes 557056 | tf_op jit(solution)/shard_map/all_gather | solution.py:56
  31.8 7.2 %copy.26 = bf16[32,512,32]{2,0,1:T(8,128)(2,1)} copy(bf16[32,512,32]{1,2,0:T(8,128)(2,1)} %fusion.9) | data formatting | bytes 2097152 | tf_op jit(solution)/shard_map/convert_element_type | solution.py:63
  39.0 7.4 %reshape.89 = bf16[16,2,16384]{2,1,0:T(2,128)(2,1)} reshape(bf16[512,32,32]{2,1,0:T(8,128)(2,1)} %bitcast.171) | data formatting | bytes 2097152
  46.5 10.4 %all-to-all-start = ((bf16[16,2,16384]{2,1,0:T(2,128)(2,1)}), bf16[16,2,16384]{2,1,0:T(2,128)(2,1)}, u32[]{:S(2)}, u32[]{:S(2)}) async-start(bf16[16,2,16384]{2,1,0:T(2,128)(2,1)} %reshape.89), calls=%async_computation | async-start | bytes 2097152 | tf_op jit(solution)/shard_map/all_to_all | solution.py:64
  59.3 39.2 %all_gather.15 = bf16[512,512]{1,0:T(8,128)(2,1)S(1)} all-gather(bf16[32,512]{1,0:T(8,128)(2,1)S(1)} %copy-done.18), channel_id=1, replica_groups=mesh['dp'=16,'seq'=16] {'dp'}, dimensions={0}, use_global_device_ids=true | all-gather | bytes 557056 | tf_op jit(solution)/shard_map/all_gather | solution.py:59
  101.1 7.2 %copy.30 = bf16[32,512,32]{2,0,1:T(8,128)(2,1)} copy(bf16[32,512,32]{1,2,0:T(8,128)(2,1)} %fusion.10) | data formatting | bytes 2097152 | tf_op jit(solution)/shard_map/convert_element_type | solution.py:83
  108.3 7.4 %reshape.93 = bf16[16,2,16384]{2,1,0:T(2,128)(2,1)} reshape(bf16[512,32,32]{2,1,0:T(8,128)(2,1)} %bitcast.172) | data formatting | bytes 2097152
  115.8 5.4 all-to-all-start.2
  124.2 39.2 %all_gather.13 = bf16[512,512]{1,0:T(8,128)(2,1)} all-gather(bf16[32,512]{1,0:T(8,128)(2,1)S(1)} %copy-done.19), channel_id=1, replica_groups=mesh['dp'=16,'seq'=16] {'dp'}, dimensions={0}, use_global_device_ids=true | all-gather | bytes 557056 | tf_op jit(solution)/shard_map/all_gather | solution.py:57
  163.5 20.2 %all_gather.14 = bf16[512,512]{1,0:T(8,128)(2,1)} all-gather(bf16[32,512]{1,0:T(8,128)(2,1)S(1)} %copy-done.20), channel_id=1, replica_groups=mesh['dp'=16,'seq'=16] {'dp'}, dimensions={0}, use_global_device_ids=true | all-gather | bytes 557056 | tf_op jit(solution)/shard_map/all_gather | solution.py:58
  183.6 6.5 reshape.90
  190.1 6.9 %copy.51 = bf16[32,16,32,32]{3,1,2,0:T(8,128)(2,1)} copy(bf16[32,16,32,32]{3,0,2,1:T(8,128)(2,1)} %bitcast.175) | data formatting | bytes 2097152 | tf_op jit(solution)/shard_map/all_to_all | solution.py:64
  197.0 6.8 all_to_all.43
  203.8 6.8 reshape.94
  214.0 8.1 %copy.31 = f32[32,32,16,32]{3,2,1,0:T(8,128)} copy(f32[32,32,16,32]{3,0,1,2:T(8,128)S(1)} %convert_bitcast_fusion) | data formatting | bytes 4194304 | tf_op jit(solution)/shard_map/convert_element_type | solution.py:85
  222.1 7.3 %reshape.76 = f32[32,32,512]{2,1,0:T(8,128)} reshape(f32[32,32,16,32]{3,2,1,0:T(8,128)} %copy.31) | data formatting | bytes 4194304 | tf_op jit(solution)/shard_map/convert_element_type | solution.py:85
  241.1 7.2 %copy.32 = bf16[32,512,32]{2,0,1:T(8,128)(2,1)} copy(bf16[32,512,32]{1,2,0:T(8,128)(2,1)} %fusion.11) | data formatting | bytes 2097152 | tf_op jit(solution)/shard_map/convert_element_type | solution.py:97
  248.3 7.5 %reshape.95 = bf16[16,2,16384]{2,1,0:T(2,128)(2,1)} reshape(bf16[512,32,32]{2,1,0:T(8,128)(2,1)} %bitcast.173) | data formatting | bytes 2097152
  255.8 6.7 all-to-all-start.3
  273.2 6.5 copy.28
  279.6 7.5 %reshape.91 = bf16[16,2,16384]{2,1,0:T(2,128)(2,1)} reshape(bf16[512,32,32]{2,1,0:T(8,128)(2,1)} %bitcast.174) | data formatting | bytes 2097152
  287.1 7.3 %all-to-all-done.3 = bf16[16,2,16384]{2,1,0:T(2,128)(2,1)} async-done(((bf16[16,2,16384]{2,1,0:T(2,128)(2,1)}), bf16[16,2,16384]{2,1,0:T(2,128)(2,1)}, u32[]{:S(2)}, u32[]{:S(2)}) %all-to-all-start.3) | async-done | bytes 1048608 | tf_op jit(solution)/shard_map/all_to_all | solution.py:99
  298.7 6.5 reshape.96
  313.1 6.8 convert_element_type.207
  326.1 6.6 reshape.92
  332.7 6.9 %copy.50 = bf16[32,16,32,32]{3,1,2,0:T(8,128)(2,1)} copy(bf16[32,16,32,32]{3,0,2,1:T(8,128)(2,1)} %bitcast.177) | data formatting | bytes 2097152 | tf_op jit(solution)/shard_map/all_to_all | solution.py:70
  339.6 5.9 all_to_all.47
  354.5 8.1 %copy.33 = f32[32,32,16,32]{3,2,1,0:T(8,128)} copy(f32[32,32,16,32]{3,0,1,2:T(8,128)S(1)} %convert_bitcast_fusion.1) | data formatting | bytes 4194304 | tf_op jit(solution)/shard_map/convert_element_type | solution.py:99
  362.7 7.4 %reshape.77 = f32[32,32,512]{2,1,0:T(8,128)} reshape(f32[32,32,16,32]{3,2,1,0:T(8,128)} %copy.33) | data formatting | bytes 4194304 | tf_op jit(solution)/shard_map/convert_element_type | solution.py:99
  374.5 63.9 %reduce-scatter.5.cloned.1.call-done = bf16[32,512]{1,0:T(8,128)(2,1)} async-done(((bf16[512,512]{1,0:T(8,128)(2,1)}), bf16[32,512]{1,0:T(8,128)(2,1)}) %reduce-scatter.5.cloned.1.call-update) | async-done | bytes 32784 | tf_op jit(solution)/shard_map/reduce_scatter | solution.py:22
  438.4 64.3 %reduce-scatter.11.cloned.1.call-done = bf16[32,512]{1,0:T(8,128)(2,1)} async-done(((bf16[512,512]{1,0:T(8,128)(2,1)}), bf16[32,512]{1,0:T(8,128)(2,1)}) %reduce-scatter.11.cloned.1.call-update) | async-done | bytes 32784 | tf_op jit(solution)/shard_map/reduce_scatter | solution.py:22
  512.2 163.4 %all-reduce.3.cloned.1.call-done = (bf16[32,512]{1,0:T(8,128)(2,1)}, bf16[32,512]{1,0:T(8,128)(2,1)}, bf16[32,512]{1,0:T(8,128)(2,1)}, bf16[32,512]{1,0:T(8,128)(2,1)}) async-done(((bf16[32,512]{1,0:T(8,128)(2,1)}, bf16[32,512]{1,0:T(8,128)(2,1)}, bf16[32,512]{1,0:T(8,128)(2,1)}, bf16[32,512]{1,0:T(8,128)(2,1)}), (bf16[32,512]{1,0:T(8,128)(2,1)}, bf16[32,512]{1,0:T(8,128)(2,1)}, bf16[32,512]{1,0:T(8,128)(2,1)}, ...) | async-done | bytes 131088 | tf_op jit(solution)/shard_map/psum | solution.py:30
  (96 shorter events, 85.5 us)
Async XLA Ops:
  7.2 1.7 copy-start.4
  8.9 0.8 copy-start.17
  9.6 20.1 %copy-start = (f32[4,8,32,512]{3,2,1,0:T(8,128)}, f32[4,8,32,512]{3,2,1,0:T(8,128)S(1)}, u32[]{:S(2)}) copy-start(f32[4,8,32,512]{3,2,1,0:T(8,128)S(1)} %copy.38) | copy-start | bytes 6291460
  29.3 0.8 copy-start.10
  29.3 0.9 copy-start.15
  46.5 69.3 %all-to-all-start = ((bf16[16,2,16384]{2,1,0:T(2,128)(2,1)}), bf16[16,2,16384]{2,1,0:T(2,128)(2,1)}, u32[]{:S(2)}, u32[]{:S(2)}) async-start(bf16[16,2,16384]{2,1,0:T(2,128)(2,1)} %reshape.89), calls=%async_computation | async-start | bytes 2097152 | tf_op jit(solution)/shard_map/all_to_all | solution.py:64
  56.8 1.7 copy-start.5
  58.5 40.4 %copy-start.1 = (f32[4,8,32,512]{3,2,1,0:T(8,128)}, f32[4,8,32,512]{3,2,1,0:T(8,128)S(1)}, u32[]{:S(2)}) copy-start(f32[4,8,32,512]{3,2,1,0:T(8,128)S(1)} %copy.36) | copy-start | bytes 6291460
  58.5 0.8 copy-start.18
  59.3 39.6 %copy-start.2 = (f32[4,8,32,512]{3,2,1,0:T(8,128)}, f32[4,8,32,512]{3,2,1,0:T(8,128)S(1)}, u32[]{:S(2)}) copy-start(f32[4,8,32,512]{3,2,1,0:T(8,128)S(1)} %copy.41) | copy-start | bytes 6291460
  98.6 0.8 copy-start.12
  115.8 88.0 %all-to-all-start.2 = ((bf16[16,2,16384]{2,1,0:T(2,128)(2,1)}), bf16[16,2,16384]{2,1,0:T(2,128)(2,1)}, u32[]{:S(2)}, u32[]{:S(2)}) async-start(bf16[16,2,16384]{2,1,0:T(2,128)(2,1)} %reshape.93), calls=%async_computation.2 | async-start | bytes 2097152 | tf_op jit(solution)/shard_map/all_to_all | solution.py:85
  121.2 3.0 copy-start.19
  121.2 42.2 %copy-start.20 = (bf16[32,512]{1,0:T(8,128)(2,1)S(1)}, bf16[32,512]{1,0:T(8,128)(2,1)}, u32[]{:S(2)}) copy-start(bf16[32,512]{1,0:T(8,128)(2,1)} %param.18) | copy-start | bytes 98308
  121.2 253.3 %reduce-scatter.9.cloned.1.call-start = ((), (), s32[]{:S(2)}) async-start(), calls=%async_computation.10 | async-start | bytes 557056 | tf_op jit(solution)/shard_map/reduce_scatter | solution.py:22
  229.5 2.2 copy-start.3
  229.5 2.2 copy-start.11
  229.5 2.2 copy-start.16
  235.5 1.0 copy-start.13
  255.8 38.5 %all-to-all-start.3 = ((bf16[16,2,16384]{2,1,0:T(2,128)(2,1)}), bf16[16,2,16384]{2,1,0:T(2,128)(2,1)}, u32[]{:S(2)}, u32[]{:S(2)}) async-start(bf16[16,2,16384]{2,1,0:T(2,128)(2,1)} %reshape.95), calls=%async_computation.3 | async-start | bytes 2097152 | tf_op jit(solution)/shard_map/all_to_all | solution.py:99
  262.5 112.1 %reduce-scatter.7.cloned.1.call-start = ((), (), s32[]{:S(2)}) async-start(), calls=%async_computation.9 | async-start | bytes 557056 | tf_op jit(solution)/shard_map/reduce_scatter | solution.py:22
  265.0 4.5 copy-start.7
  265.8 3.7 copy-start.14
  294.3 31.8 %all-to-all-start.1 = ((bf16[16,2,16384]{2,1,0:T(2,128)(2,1)}), bf16[16,2,16384]{2,1,0:T(2,128)(2,1)}, u32[]{:S(2)}, u32[]{:S(2)}) async-start(bf16[16,2,16384]{2,1,0:T(2,128)(2,1)} %reshape.91), calls=%async_computation.1 | async-start | bytes 2097152 | tf_op jit(solution)/shard_map/all_to_all | solution.py:70
  298.7 139.7 %reduce-scatter.5.cloned.1.call-start = ((), (), s32[]{:S(2)}) async-start(), calls=%async_computation.8 | async-start | bytes 557056 | tf_op jit(solution)/shard_map/reduce_scatter | solution.py:22
  319.9 3.4 copy-start.6
  323.1 179.6 %reduce-scatter.11.cloned.1.call-start = ((), (), s32[]{:S(2)}) async-start(), calls=%async_computation.11 | async-start | bytes 557056 | tf_op jit(solution)/shard_map/reduce_scatter | solution.py:22
  348.3 327.2 %all-reduce.3.cloned.1.call-start = ((), (), s32[]{:S(2)}) async-start(), calls=%async_computation.12 | async-start | bytes 262144 | tf_op jit(solution)/shard_map/psum | solution.py:30
  502.7 3.2 copy-start.9
  505.9 1.6 copy-start.8
Sparse Core Ops, SparseCore 0:
  238.2 60.8 reduce-scatter.8
  301.7 72.3 reduce-scatter.6
  377.2 61.1 reduce-scatter.4
  441.5 61.1 reduce-scatter.10
  505.4 170.1 all-reduce.2
where the time goes:
time: 698 us; the launch traced here: 688 us
  waiting for transfers between devices  299 us (43%)
  local copies, waits for them, and re-layouts  178 us (26%)
  blocking collectives  118 us (17%)
  matrix products  31.2 us (4%)
  starting transfers between devices  27.2 us (4%)
  other arithmetic  20.2 us (3%)
  between operations  14.5 us (2%)
    psum x1, waiting for transfers between devices, reduce_factor(): return lax.psum(owned, 'seq').astype(jnp.float32)  163 us
    reduce_scatter x4, waiting for transfers between devices, reduce_factor(): lax.psum_scatter(term(jnp.int32(0), total_rows // lax.axis_size('dp') * l...  128 us
    unnamed x62, local copies, waits for them, and re-layouts  78.7 us
    all_gather x1, blocking collectives, shards(): lax.all_gather(left_out, 'dp', axis=0, tiled=True)  39.2 us
    all_gather x1, blocking collectives, shards(): lax.all_gather(left_in, 'dp', axis=0, tiled=True)  39.2 us
    all_gather x1, blocking collectives, shards(): lax.all_gather(right_out, 'dp', axis=0, tiled=True)  20.2 us
    all_gather x1, blocking collectives, shards(): lax.all_gather(right_in, 'dp', axis=0, tiled=True)  19.7 us
    convert_element_type x2, local copies, waits for them, and re-layouts, shards(): lax.all_to_all(back_one, 'seq', split_axis=1, concat_axis=2, tiled=True)  15.5 us
  transfers between devices with their start and end apart: 9, of which 4 were waited for; matrix products, arithmetic and copies ran while one was open for 23% of the time, Pallas kernels for 0%

commit v1 on v0

v1 whole, which is shorter than its diff:
```python
import math

import jax
import jax.numpy as jnp
from jax import lax
from jax.experimental import pallas as pl
from jax.experimental.pallas import tpu as pltpu
from jax.sharding import PartitionSpec as P

C = 512
NB = 512
BS = 512
SCALE = 1.0 / math.sqrt(C * NB)
BF = jnp.bfloat16
F32 = jnp.float32
NT = (((1,), (1,)), ((), ()))
NN = (((1,), (0,)), ((), ()))
TN = (((0,), (0,)), ((), ()))
R1, L2, L1, R2 = 0, 1, 2, 3
T1, DT2, T2, DT1 = 0, 1, 2, 3
GRO, GLI, GLO, GRI = 0, 1, 2, 3


def dot(a, b, dims):
    return lax.dot_general(a, b, dims, preferred_element_type=F32)


def mixer(
    q_hbm, k_hbm, v_hbm, h_hbm, g_hbm, rin, lin, rout, lout, tw1, tw2,
    mo_hbm, gq_hbm, gk_hbm, gv_hbm, gh_hbm, gri_out, gli_out, gro_out, glo_out,
    qn, kn, vn, hn, gn,
    us, gos, hs, zs, fac, fact, t1x, wx, ds2x, dzx, t2x, ds1x,
    sbuf, rbuf, perm_in, perm_out, regroup, tw1x, tw2x, tw1t, tw2t, nat,
    gb, gc, xs, xr, zb, zr, yr,
    load_sem, out_sem, fs_sem, fr_sem, as_sem, ar_sem,
    gcs_sem, gcr_sem, xs_sem, xr_sem, zs_sem, zr_sem, ys_sem, yr_sem,
):
    dp = lax.axis_index("dp")
    me = lax.axis_index("seq")
    x, zl, co = dp // 4, (dp // 2) % 2, dp % 2
    y, zh = me // 4, me % 4

    def device(dx, dl, dc, dy, dh):
        return {
            "dp": ((x + dx) % 4) * 4 + ((zl + dl) % 2) * 2 + (co + dc) % 2,
            "seq": ((y + dy) % 4) * 4 + (zh + dh) % 4,
        }

    def remote(src, dst, ssem, rsem, to):
        return pltpu.make_async_remote_copy(
            src_ref=src, dst_ref=dst, send_sem=ssem, recv_sem=rsem,
            device_id=to, device_id_type=pl.DeviceIdType.MESH,
        )

    def load(n, hbm, vmem):
        @pl.loop(0, 32)
        def _(i):
            pltpu.make_async_copy(
                hbm.at[:, pl.ds(pl.multiple_of(i * 512, 512), 512)], vmem.at[i], load_sem.at[n]
            ).start()

    def load_wait(n, vmem):
        pltpu.make_async_copy(vmem, vmem, load_sem.at[n]).wait()

    def store(n, hbm, vmem):
        @pl.loop(0, 32)
        def _(i):
            pltpu.make_async_copy(
                vmem.at[i], hbm.at[:, pl.ds(pl.multiple_of(i * 512, 512), 512)], out_sem.at[n]
            ).start()

    def store_wait(n, vmem):
        pltpu.make_async_copy(vmem, vmem, out_sem.at[n]).wait()

    peers = (
        [(0, 0, 0, dy, dh) for dy in range(4) for dh in range(4) if dy or dh]
        + [(dx, 0, 0, dy, 0) for dx in range(1, 4) for dy in range(4)]
        + [(0, 1, 0, 0, dh) for dh in range(4)]
        + [(0, 0, 1, 0, 0)]
    )
    barrier = pltpu.get_barrier_semaphore()
    for offset in peers:
        pl.semaphore_signal(
            barrier, inc=1, device_id=device(*offset), device_id_type=pl.DeviceIdType.MESH
        )
    load(0, k_hbm, kn)
    load(1, v_hbm, vn)
    load(2, g_hbm, gn)
    load(3, q_hbm, qn)
    load(4, h_hbm, hn)

    def grid2(shape, hold):
        r = lax.broadcasted_iota(jnp.int32, shape, 0)
        q = lax.broadcasted_iota(jnp.int32, shape, 1)
        return jnp.where(hold(r, q), 1.0, 0.0).astype(BF)

    perm_in[...] = grid2((512, 512), lambda r, q: (r >> 4 == (q & 31)) & ((r & 15) == q >> 5))
    pl.semaphore_wait(barrier, len(peers))

    def fcopy(f, block, to):
        return remote(fac.at[f, block], fac.at[f, block], fs_sem.at[f, block, 0], fr_sem.at[f, block], to)

    xpeers = (2, 1, 3)
    zblock = x * 4 + (1 - zl) * 2 + co

    def fsend(f, block, slot, to):
        remote(
            fac.at[f, block], fac.at[f, block], fs_sem.at[f, block, slot], fr_sem.at[f, block], to
        ).start()

    def fwait_send(f, block, slot):
        remote(
            fac.at[f, block], fac.at[f, block], fs_sem.at[f, block, slot], fr_sem.at[f, block],
            device(0, 0, 1, 0, 0),
        ).wait_send()

    def fwait(f, block):
        remote(
            fac.at[f, block], fac.at[f, block], fs_sem.at[f, block, 0], fr_sem.at[f, block],
            device(0, 0, 1, 0, 0),
        ).wait_recv()

    def gather_a(f, ref):
        fac[f, dp] = ref[...]
        fsend(f, dp, 4, device(0, 1, 0, 0, 0))
        for dx in xpeers:
            fsend(f, dp, dx, device(dx, 0, 0, 0, 0))
        fsend(f, dp, 0, device(0, 0, 1, 0, 0))

    def gather_b(f):
        fwait(f, zblock)
        for dx in xpeers:
            fsend(f, zblock, dx, device(dx, 0, 0, 0, 0))
        fsend(f, zblock, 0, device(0, 0, 1, 0, 0))

    def gather_c(f):
        for dl in range(2):
            for dx in (1, 3, 2):
                block = ((x + dx) % 4) * 4 + ((zl + dl) % 2) * 2 + co
                fwait(f, block)
                fsend(f, block, 0, device(0, 0, 1, 0, 0))

    def gather_d(f):
        @pl.loop(0, 8)
        def _(b):
            fwait(f, b * 2 + 1 - co)

    def gather_end(f):
        for dx in xpeers:
            fwait_send(f, dp, dx)
            fwait_send(f, zblock, dx)
        fwait_send(f, dp, 4)

        @pl.loop(0, 8)
        def _(b):
            fwait_send(f, b * 2 + co, 0)

    def factor(f):
        return fac[f].reshape(512, 512)

    def shuffle(src, dst):
        @pl.loop(0, 2)
        def _(n):
            block = src[pl.ds(n * 16, 16)].reshape(512, 512)
            dst[:, pl.ds(pl.multiple_of(n * 16, 16), 16), :] = (
                dot(perm_in[...], block, NN).astype(BF).reshape(32, 16, 512)
            )

    def product(a, b, dst):
        @pl.loop(0, 32)
        def _(i):
            dst[i] = (a[i].astype(F32) * b[i].astype(F32)).astype(BF)

    def exchange_send(n):
        for dy in range(4):
            for dh in (2, 1, 3, 0):
                if dy or dh:
                    to = ((y + dy) % 4) * 4 + (zh + dh) % 4
                    remote(
                        sbuf.at[n, to], rbuf.at[n, me], as_sem.at[n, to], ar_sem.at[n, me],
                        device(0, 0, 0, dy, dh),
                    ).start()
        rbuf[n, me] = sbuf[n, me]

    def exchange_wait_send(n):
        for dy in range(4):
            for dh in (2, 1, 3, 0):
                if dy or dh:
                    to = ((y + dy) % 4) * 4 + (zh + dh) % 4
                    remote(
                        sbuf.at[n, to], rbuf.at[n, me], as_sem.at[n, to], ar_sem.at[n, me],
                        device(0, 0, 0, dy, dh),
                    ).wait_send()

    def exchange_wait_recv(n, dy):
        for dh in (2, 1, 3, 0):
            if dy or dh:
                source = ((y - dy + 4) % 4) * 4 + (zh - dh + 4) % 4
                remote(
                    sbuf.at[n, source], rbuf.at[n, source], as_sem.at[n, source],
                    ar_sem.at[n, source], device(0, 0, 0, dy, dh),
                ).wait_recv()

    def arrange(n, dst, twist):
        for dy in range(4):
            exchange_wait_recv(n, dy)
            yg = (y - dy + 4) % 4
            lhs = jnp.concatenate(
                [
                    jnp.concatenate(
                        [rbuf[n, yg * 4 + b, :, ch * 128 : ch * 128 + 128] for b in range(4)], axis=1
                    )
                    for ch in range(8)
                ],
                axis=0,
            )
            lanes = pl.ds(pl.multiple_of(yg * 128, 128), 128)
            out = dot(lhs, regroup[...], NN)
            for ch in range(8):
                for cl in range(4):
                    piece = out[ch * 32 : ch * 32 + 32, cl * 128 : cl * 128 + 128]
                    if twist is not None:
                        piece = piece * twist[:, lanes]
                    dst[ch * 4 + cl, :, lanes] = piece.astype(BF)

    def spread(n, left, right, twist):
        @pl.loop(0, 4)
        def _(m):
            out = dot(left, right[pl.ds(m * 8, 8)].reshape(256, 512), NT)
            for part in range(2):
                piece = out[:, part * 128 : part * 128 + 128]
                if twist is not None:
                    piece = piece * twist[...]
                lanes = pl.ds(pl.multiple_of(m * 256 + part * 128, 128), 128)
                sbuf[n, :, :, lanes] = piece.astype(BF).reshape(16, 32, 128)

    def share(n, first, second):
        @pl.loop(0, 4)
        def _(m):
            lanes = pl.ds(pl.multiple_of(m * 128, 128), 128)
            out = dot(first[:, :, lanes].reshape(1024, 128), second[...].reshape(1024, 512), TN)
            out = out.astype(BF)
            for p in range(4):
                gb[n, p % 2, m * 2 + p // 2] = out[p * 32 : p * 32 + 32]

    def core_copy(n):
        return remote(
            gb.at[n, 1 - co], gc.at[n], gcs_sem.at[n], gcr_sem.at[n], device(0, 0, 1, 0, 0)
        )

    def core_send(n):
        core_copy(n).start()

    def xy_copy(n, dx, dy):
        to = ((x + dx) % 4) * 4 + (y + dy) % 4
        return remote(
            xs.at[n, to], xr.at[n, x * 4 + y], xs_sem.at[n, to], xr_sem.at[n, x * 4 + y],
            device(dx, 0, 0, dy, 0),
        )

    XY = [(dx, dy) for dx in (2, 1, 3, 0) for dy in (2, 1, 3, 0) if dx or dy]

    def xy_send(n):
        core_copy(n).wait_recv()

        @pl.loop(0, 4)
        def _(m):
            total = gb[n, co, pl.ds(m * 2, 2)].astype(F32) + gc[n, pl.ds(m * 2, 2)].astype(F32)
            total = total.astype(BF).reshape(64, 512)
            for p in range(4):
                xs[n, m * 4 + p] = total[:, p * 128 : p * 128 + 128]

        for dx, dy in XY:
            xy_copy(n, dx, dy).start()
        xr[n, x * 4 + y] = xs[n, x * 4 + y]

    def z_copy(n, dh, dl):
        z = zh * 2 + zl
        to = ((zh + dh) % 4) * 2 + (zl + dl) % 2
        return remote(
            zb.at[n, (zl + dl) % 2], zr.at[n, z], zs_sem.at[n, to], zr_sem.at[n, z],
            device(0, dl, 0, 0, dh),
        )

    Z = [(dh, dl) for dh in (2, 1, 3, 0) for dl in range(2) if dh or dl]

    def z_send(n):
        for dx, dy in XY:
            source = ((x - dx + 4) % 4) * 4 + (y - dy + 4) % 4
            remote(
                xs.at[n, source], xr.at[n, source], xs_sem.at[n, source], xr_sem.at[n, source],
                device(dx, 0, 0, dy, 0),
            ).wait_recv()
        total = xr[n, 0].astype(F32)
        for p in range(1, 16):
            total = total + xr[n, p].astype(F32)
        zb[n] = total.astype(BF).reshape(2, 32, 128)
        for dh, dl in Z:
            z_copy(n, dh, dl).start()
        zr[n, zh * 2 + zl] = zb[n, zl]

    def y_copy(n, dy):
        return remote(
            yr.at[n, y], yr.at[n, y], ys_sem.at[n, dy], yr_sem.at[n, y], device(0, 0, 0, dy, 0)
        )

    def y_send(n):
        for dh, dl in Z:
            source = ((zh - dh + 4) % 4) * 2 + (zl - dl + 2) % 2
            remote(
                zb.at[n, 0], zr.at[n, source], zs_sem.at[n, source], zr_sem.at[n, source],
                device(0, dl, 0, 0, dh),
            ).wait_recv()
        total = zr[n, 0].astype(F32)
        for p in range(1, 8):
            total = total + zr[n, p].astype(F32)
        yr[n, y] = total * SCALE
        for dy in (2, 1, 3):
            y_copy(n, dy).start()

    def finish(n, out):
        for dy in (2, 1, 3):
            source = (y - dy + 4) % 4
            remote(
                yr.at[n, source], yr.at[n, source], ys_sem.at[n, dy], yr_sem.at[n, source],
                device(0, 0, 0, dy, 0),
            ).wait_recv()
        for p in range(4):
            out[:, p * 128 : p * 128 + 128] = yr[n, p]

    def reduce_end(n):
        core_copy(n).wait_send()
        for dx, dy in XY:
            xy_copy(n, dx, dy).wait_send()
        for dh, dl in Z:
            z_copy(n, dh, dl).wait_send()
        for dy in (2, 1, 3):
            y_copy(n, dy).wait_send()

    def outputs(left, f, dims, first, second, swap):
        @pl.loop(0, 2)
        def _(n):
            rows = pl.ds(pl.multiple_of(n * 16, 16), 16)
            out = dot(left[:, rows, :].reshape(512, 512), factor(f), dims).astype(BF)
            nat[...] = dot(perm_out[...], out, NN).reshape(16, 32, 512)

            @pl.loop(0, 16)
            def _(i):
                value = nat[i]
                a = first[n * 16 + i].astype(F32)
                b = second[n * 16 + i].astype(F32)
                first[n * 16 + i] = (value * (b if swap else a)).astype(BF)
                second[n * 16 + i] = (value * (a if swap else b)).astype(BF)

    gather_a(R1, rin)
    load_wait(0, kn)
    load_wait(1, vn)
    product(kn, vn, wx)
    shuffle(wx, us)
    gather_b(R1)
    tw1x[...] = jnp.concatenate([tw1[...]] * 4, axis=1)
    tw2x[...] = jnp.concatenate([tw2[...]] * 4, axis=1)
    gather_c(R1)
    gather_d(R1)
    fact[0] = factor(R1).T
    spread(T1, fact[0], us, tw1x)
    exchange_send(T1)

    for f, ref in ((L2, lout), (L1, lin), (R2, rout)):
        gather_a(f, ref)
    load_wait(2, gn)
    load_wait(3, qn)
    product(gn, qn, wx)
    shuffle(wx, gos)
    for f in (L2, L1, R2):
        gather_b(f)
    regroup[...] = grid2(
        (512, 512),
        lambda r, q: (r >> 7 == ((q >> 5) & 3)) & (((r >> 5) & 3) == q >> 7) & ((r & 31) == (q & 31)),
    )
    perm_out[...] = grid2((512, 512), lambda q, r: (r >> 4 == (q & 31)) & ((r & 15) == q >> 5))
    tw1t[...] = tw1[...].T
    tw2t[...] = tw2[...].T
    for f in (L2, L1, R2):
        gather_c(f)
    load_wait(4, hn)
    shuffle(hn, hs)
    for f in (L2, L1, R2):
        gather_d(f)
    spread(DT2, factor(L2), gos, None)
    fact[1] = factor(R2).T
    exchange_wait_send(T1)
    exchange_send(DT2)

    arrange(T1, t1x, None)

    @pl.loop(0, 4)
    def _(m):
        rows = pl.ds(m * 8, 8)
        out = dot(t1x[rows].reshape(256, 512), factor(L1), NN).reshape(8, 32, 512)
        zs[rows] = out
        wx[rows] = (out * hs[rows].astype(F32)).astype(BF)

    spread(T2, fact[1], wx, tw2x)
    exchange_wait_send(DT2)
    exchange_send(T2)

    arrange(DT2, ds2x, tw2t)

    @pl.loop(0, 2)
    def _(n):
        rows = pl.ds(pl.multiple_of(n * 16, 16), 16)
        out = dot(ds2x[:, rows, :].reshape(512, 512), factor(R2), NT).reshape(32, 16, 512)
        dzx[:, rows, :] = (out * hs[:, rows, :].astype(F32)).astype(BF)
        grad = (out * zs[:, rows, :]).astype(BF).reshape(512, 512)
        hn[pl.ds(n * 16, 16)] = dot(perm_out[...], grad, NN).astype(BF).reshape(16, 32, 512)

    spread(DT1, factor(L1), dzx, None)
    store(4, gh_hbm, hn)
    share(GRO, wx, ds2x)
    core_send(GRO)
    share(GLI, t1x, dzx)
    core_send(GLI)
    xy_send(GRO)
    xy_send(GLI)
    exchange_wait_send(T2)
    exchange_send(DT1)
    z_send(GRO)
    z_send(GLI)

    arrange(T2, t2x, None)
    share(GLO, t2x, gos)
    core_send(GLO)
    outputs(t2x, L2, NN, qn, gn, False)
    store(0, mo_hbm, qn)
    store(1, gq_hbm, gn)
    xy_send(GLO)
    y_send(GRO)
    y_send(GLI)
    z_send(GLO)
    finish(GRO, gro_out)
    finish(GLI, gli_out)
    y_send(GLO)

    arrange(DT1, ds1x, tw1t)
    share(GRI, us, ds1x)
    core_send(GRI)
    finish(GLO, glo_out)
    xy_send(GRI)
    outputs(ds1x, R1, NT, kn, vn, True)
    store(2, gk_hbm, kn)
    store(3, gv_hbm, vn)
    z_send(GRI)
    exchange_wait_send(DT1)
    for f in range(4):
        gather_end(f)
    for n in (GRO, GLI, GLO):
        reduce_end(n)
    y_send(GRI)
    for n, vmem in enumerate((qn, gn, kn, vn, hn)):
        store_wait(n, vmem)
    finish(GRI, gri_out)
    reduce_end(GRI)


def shards(*args):
    any_spec = pl.BlockSpec(memory_space=pl.ANY)
    vmem_spec = pl.BlockSpec(memory_space=pltpu.VMEM)
    stream = pltpu.VMEM((32, 32, 512), BF)
    dma = pltpu.SemaphoreType.DMA
    outs = pl.pallas_call(
        mixer,
        out_shape=[jax.ShapeDtypeStruct((32, 16384), BF)] * 5
        + [jax.ShapeDtypeStruct((32, 512), F32)] * 4,
        in_specs=[any_spec] * 5 + [vmem_spec] * 6,
        out_specs=[any_spec] * 5 + [vmem_spec] * 4,
        scratch_shapes=[stream] * 5
        + [stream] * 3
        + [pltpu.VMEM((32, 32, 512), F32)]
        + [pltpu.VMEM((4, 16, 32, 512), BF), pltpu.VMEM((2, 512, 512), BF)]
        + [stream] * 6
        + [pltpu.VMEM((4, 16, 32, 1024), BF)] * 2
        + [pltpu.VMEM((512, 512), BF)] * 3
        + [pltpu.VMEM((512, 128), F32)] * 2
        + [pltpu.VMEM((32, 512), F32)] * 2
        + [pltpu.VMEM((16, 32, 512), F32)]
        + [
            pltpu.VMEM((4, 2, 8, 32, 512), BF),
            pltpu.VMEM((4, 8, 32, 512), BF),
            pltpu.VMEM((4, 16, 64, 128), BF),
            pltpu.VMEM((4, 16, 64, 128), BF),
            pltpu.VMEM((4, 2, 32, 128), BF),
            pltpu.VMEM((4, 8, 32, 128), BF),
            pltpu.VMEM((4, 4, 32, 128), F32),
        ]
        + [
            dma((5,)), dma((5,)), dma((4, 16, 5)), dma((4, 16)), dma((4, 16)), dma((4, 16)),
            dma((4,)), dma((4,)), dma((4, 16)), dma((4, 16)), dma((4, 8)), dma((4, 8)),
            dma((4, 4)), dma((4, 4)),
        ],
        compiler_params=pltpu.CompilerParams(
            collective_id=0, has_side_effects=True, vmem_limit_bytes=60 << 20
        ),
        cost_estimate=pl.CostEstimate(
            flops=13_000_000_000, bytes_accessed=12 << 20, transcendentals=0
        ),
        name="mixer",
    )(*args)
    return tuple(outs)


def solution(mesh):
    wide, rows, cols = P("dp", "seq"), P("dp", None), P(None, "seq")
    return jax.shard_map(
        shards,
        mesh=mesh,
        in_specs=(wide,) * 5 + (rows,) * 4 + (cols,) * 2,
        out_specs=(wide,) * 5 + (rows,) * 4,
        check_vma=False,
    )
```

time: 698 us -> 177 us (0.25); the launches traced: 688 us -> 175 us
  waiting for transfers between devices: 299 us -> 0 us
  local copies, waits for them, and re-layouts: 178 us -> 13.9 us
  Pallas kernels: 0 us -> 161 us
  blocking collectives: 118 us -> 0 us
  matrix products: 31.2 us -> 0 us
  starting transfers between devices: 27.2 us -> 0 us
  other arithmetic: 20.2 us -> 0 us
  between operations: 14.5 us -> 0.68 us
    psum x1 -> x0, waiting for transfers between devices: 163 us -> none  [reduce_factor(): return lax.psum(owned, 'seq').astype(jnp.float32)]
    pallas_call x0 -> x1, Pallas kernels: none -> 161 us  [shards(): pl.pallas_call(mixer, out_shape=[jax.ShapeDtypeStruct((32, 16384), BF)] *...]
    reduce_scatter x4 -> x0, waiting for transfers between devices: 128 us -> none  [reduce_factor(): lax.psum_scatter(term(jnp.int32(0), total_rows // lax.axis_size('dp') * l...]
    all_gather x4 -> x0, blocking collectives: 118 us -> none  [the longest x1 39.2 us: shards(): lax.all_gather(left_out, 'dp', axis=0, tiled=True)]
    convert_element_type x10 -> x0, local copies, waits for them, and re-layouts: 70.5 us -> none  [the longest x2 15.5 us: shards(): lax.all_to_all(back_one, 'seq', split_axis=1, concat_axis=2, tiled=True)]
    unnamed x62 -> x29, local copies, waits for them, and re-layouts: 78.7 us -> 13.9 us
    dot_general x12 -> x0, matrix products: 31.2 us -> none  [the longest x4 9.01 us: term(): jnp.einsum(form, first, second, preferred_element_type=jnp.float32) * scale]
    all_to_all x4 -> x0, starting transfers between devices: 26.8 us -> none  [the longest x1 10.4 us: shards(): lax.all_to_all(twisted, 'seq', split_axis=1, concat_axis=2, tiled=True)]
  transfers between devices with their start and end apart: 9 -> 0, of which waited for: 4 -> 0; matrix products, arithmetic and copies ran while one was open for 23% -> 0% of each run, Pallas kernels for 0% -> 0%
where the time goes in v1:
time: 177 us; the launch traced here: 175 us
  Pallas kernels  161 us (91%)
  local copies, waits for them, and re-layouts  13.9 us (8%)
    pallas_call x1, Pallas kernels, shards(): pl.pallas_call(mixer, out_shape=[jax.ShapeDtypeStruct((32, 16384), BF)] *...  161 us
    unnamed x29, local copies, waits for them, and re-layouts  13.9 us

profile of v1, /device:TPU:2, one launch (start us, length us, event | category | flops | bytes accessed | tf_op | source)
XLA Modules:
  0.0 175.3 jit_solution(6955795761309907312)
XLA Ops:
  0.6 0.0 copy-start.4
  0.7 1.7 copy.20.tw1
  2.4 0.0 copy-done.4
  2.4 0.8 copy.21.tw2
  3.2 160.8 %mixer.1 = (bf16[32,16384]{1,0:T(8,128)(2,1)}, bf16[32,16384]{1,0:T(8,128)(2,1)}, bf16[32,16384]{1,0:T(8,128)(2,1)}, bf16[32,16384]{1,0:T(8,128)(2,1)}, bf16[32,...) custom-call(bf16[32,16384]{1,0:T(8,128)(2,1)} %q_hbm.1, ...), custom_call_target="tpu_custom_call" | custom-call | flops 12999999488 | bytes 12582912 | tf_op jit(solution)/shard_map/mixer/pallas_call | solution.py:471
  164.0 0.0 copy-start.3
  164.0 2.4 %copy.31 = bf16[32,16384]{1,0:T(8,128)(2,1)} copy(bf16[32,16384]{1,0:T(8,128)(2,1)} %get-tuple-element.18) | data formatting | bytes 2097152
  166.3 0.0 copy-done.3
  166.3 0.0 copy-start.2
  166.3 1.0 copy.32
  167.3 0.6 copy-done.2
  167.9 0.0 copy-start.1
  167.9 1.0 copy.33
  168.9 0.6 copy-done.1
  169.5 0.0 copy-start
  169.5 1.0 copy.34
  170.5 0.6 copy-done
  171.1 0.0 copy-start.8
  171.1 1.0 copy.35
  172.1 0.0 copy-done.8
  172.1 0.0 copy-start.7
  172.1 0.6 copy.36
  172.8 0.2 copy-done.7
  173.0 0.0 copy-start.6
  173.0 0.6 copy.37
  173.6 0.2 copy-done.6
  173.8 0.0 copy-start.5
  173.8 0.6 copy.38
  174.5 0.2 copy-done.5
  174.7 0.6 copy.39
Async XLA Ops:
  0.6 1.7 copy-start.4
  164.0 2.4 %copy-start.3 = (bf16[32,16384]{1,0:T(8,128)(2,1)S(1)}, bf16[32,16384]{1,0:T(8,128)(2,1)}, u32[]{:S(2)}) copy-start(bf16[32,16384]{1,0:T(8,128)(2,1)} %get-tuple-element.19) | copy-start | bytes 3145732
  166.3 1.6 copy-start.2
  167.9 1.6 copy-start.1
  169.5 1.6 copy-start
  171.1 1.0 copy-start.8
  172.1 0.9 copy-start.7
  173.0 0.9 copy-start.6
  173.8 0.9 copy-start.5

commit v2 on v1

v2 whole, which is shorter than its diff:
```python
import math

import jax
import jax.numpy as jnp
from jax import lax
from jax.experimental import pallas as pl
from jax.experimental.pallas import tpu as pltpu
from jax.sharding import PartitionSpec as P

C = 512
NB = 512
BS = 512
SCALE = 1.0 / math.sqrt(C * NB)
BF = jnp.bfloat16
F32 = jnp.float32
NT = (((1,), (1,)), ((), ()))
NN = (((1,), (0,)), ((), ()))
TN = (((0,), (0,)), ((), ()))
R1, L2, L1, R2 = 0, 1, 2, 3
T1, DT2, T2, DT1 = 0, 1, 2, 3
GRO, GLI, GLO, GRI = 0, 1, 2, 3
WINDOW = 4
YORDER = (1, 2, 3, 0)
PARTS = 4


def dot(a, b, dims):
    return lax.dot_general(a, b, dims, preferred_element_type=F32)


def mixer(
    q_hbm, k_hbm, v_hbm, h_hbm, g_hbm, rin, lin, rout, lout, tw1_hbm, tw2_hbm,
    o_hbm, du_hbm, gh_hbm, grads_hbm,
    qn, kn, vn, hn, gn,
    us, gos, hs, zs, fac, fact, t1x, wx, ds2x, dzx, t2x, ds1x,
    sbuf, rbuf, perm_in, perm_out, regroup, tw1x, tw2x, tw1t, tw2t,
    gb, gc, xs, xr, zb, zr, yr, grads,
    load_sem, own_sem, out_sem, fs_sem, fr_sem, as_sem, ar_sem,
    gcs_sem, gcr_sem, xs_sem, xr_sem, zs_sem, zr_sem, ys_sem, yr_sem,
):
    dp = lax.axis_index("dp")
    me = lax.axis_index("seq")
    x, zl, co = dp // 4, (dp // 2) % 2, dp % 2
    y, zh = me // 4, me % 4

    def device(dx, dl, dc, dy, dh):
        return {
            "dp": ((x + dx) % 4) * 4 + ((zl + dl) % 2) * 2 + (co + dc) % 2,
            "seq": ((y + dy) % 4) * 4 + (zh + dh) % 4,
        }

    def remote(src, dst, ssem, rsem, to):
        return pltpu.make_async_remote_copy(
            src_ref=src, dst_ref=dst, send_sem=ssem, recv_sem=rsem,
            device_id=to, device_id_type=pl.DeviceIdType.MESH,
        )

    def load(n, hbm, vmem):
        @pl.loop(0, 32)
        def _(i):
            pltpu.make_async_copy(
                hbm.at[:, pl.ds(pl.multiple_of(i * 512, 512), 512)], vmem.at[i], load_sem.at[n]
            ).start()

    def load_wait(n, vmem):
        pltpu.make_async_copy(vmem, vmem, load_sem.at[n]).wait()

    def store(n, hbm, vmem):
        @pl.loop(0, 32)
        def _(i):
            pltpu.make_async_copy(
                vmem.at[i], hbm.at[:, pl.ds(pl.multiple_of(i * 512, 512), 512)], out_sem.at[n]
            ).start()

    def store_wait(n, vmem):
        pltpu.make_async_copy(vmem, vmem, out_sem.at[n]).wait()

    peers = (
        [(0, 0, 0, dy, dh) for dy in range(4) for dh in range(4) if dy or dh]
        + [(dx, 0, 0, dy, 0) for dx in range(1, 4) for dy in range(4)]
        + [(0, 1, 0, 0, dh) for dh in range(4)]
        + [(dx, 1, 0, 0, 0) for dx in range(1, 4)]
        + [(0, 0, 1, 0, 0)]
    )
    barrier = pltpu.get_barrier_semaphore()
    for offset in peers:
        pl.semaphore_signal(
            barrier, inc=1, device_id=device(*offset), device_id_type=pl.DeviceIdType.MESH
        )
    own = (rin, lout, lin, rout)
    twist_loads = (
        pltpu.make_async_copy(tw1_hbm, tw1t, own_sem.at[4]),
        pltpu.make_async_copy(tw2_hbm, tw2t, own_sem.at[5]),
    )
    for f in range(4):
        pltpu.make_async_copy(own[f], fac.at[f, dp], own_sem.at[f]).start()
    load(0, k_hbm, kn)
    load(1, v_hbm, vn)
    for copy in twist_loads:
        copy.start()
    load(2, g_hbm, gn)
    load(3, q_hbm, qn)
    load(4, h_hbm, hn)

    def grid2(shape, hold):
        r = lax.broadcasted_iota(jnp.int32, shape, 0)
        q = lax.broadcasted_iota(jnp.int32, shape, 1)
        return jnp.where(hold(r, q), 1.0, 0.0).astype(BF)

    perm_in[...] = grid2((512, 512), lambda r, q: (r >> 4 == (q & 31)) & ((r & 15) == q >> 5))
    pl.semaphore_wait(barrier, len(peers))

    CORE = device(0, 0, 1, 0, 0)
    zblock = x * 4 + (1 - zl) * 2 + co

    def fsend(f, block, slot, to):
        remote(fac.at[f, block], fac.at[f, block], fs_sem.at[0], fr_sem.at[f, slot], to).start()

    def fwait(f, slot, count):
        blocks = fac.at[f, pl.ds(0, count)]
        remote(blocks, blocks, fs_sem.at[0], fr_sem.at[f, slot], CORE).wait_recv()

    def fslot(dx):
        return 1 + dx

    def gather_a(f, direct):
        pltpu.make_async_copy(own[f], fac.at[f, dp], own_sem.at[f]).wait()
        fsend(f, dp, fslot(0), device(0, 1, 0, 0, 0))
        for dx in (2, 1, 3):
            fsend(f, dp, fslot(dx), device(dx, 0, 0, 0, 0))
            if direct:
                fsend(f, dp, fslot(dx), device(dx, 1, 0, 0, 0))
        fsend(f, dp, 0, CORE)

    def gather_b(f, direct):
        fwait(f, fslot(0), 1)
        if not direct:
            for dx in (2, 1, 3):
                fsend(f, zblock, fslot(dx), device(dx, 0, 0, 0, 0))
        fsend(f, zblock, 0, CORE)

    def gather_c(f):
        for dx in (1, 3, 2):
            fwait(f, fslot(dx), 2)
            for side in range(2):
                fsend(f, ((x - dx + 4) % 4) * 4 + side * 2 + co, 0, CORE)

    def gather_d(f):
        fwait(f, 0, 8)

    def gather_end():
        blocks = fac.at[:, pl.ds(0, 15)]
        remote(blocks, blocks, fs_sem.at[0], fr_sem.at[0, 0], CORE).wait_send()

    def factor(f):
        return fac[f].reshape(512, 512)

    def shuffle(src, dst):
        @pl.loop(0, 2)
        def _(n):
            block = src[pl.ds(n * 16, 16)].reshape(512, 512)
            dst[:, pl.ds(pl.multiple_of(n * 16, 16), 16), :] = (
                dot(perm_in[...], block, NN).astype(BF).reshape(32, 16, 512)
            )

    def product(a, b, dst):
        @pl.loop(0, 32)
        def _(i):
            dst[i] = (a[i].astype(F32) * b[i].astype(F32)).astype(BF)

    pending = []

    def exchange_group(dy):
        return [(dy, dh) for dh in (2, 1, 3, 0) if dy or dh]

    def exchange_wait_send(n, dy):
        blocks = sbuf.at[n, pl.ds(0, len(exchange_group(dy)))]
        remote(blocks, blocks, as_sem.at[n, dy], ar_sem.at[n, dy], CORE).wait_send()

    def exchange_send(n):
        rbuf[n, me] = sbuf[n, me]
        for dy in YORDER:
            if len(pending) == WINDOW:
                exchange_wait_send(*pending.pop(0))
            for _, dh in exchange_group(dy):
                to = ((y + dy) % 4) * 4 + (zh + dh) % 4
                remote(
                    sbuf.at[n, to], rbuf.at[n, me], as_sem.at[n, dy], ar_sem.at[n, dy],
                    device(0, 0, 0, dy, dh),
                ).start()
            pending.append((n, dy))

    def exchange_end():
        while pending:
            exchange_wait_send(*pending.pop(0))

    def exchange_wait_recv(n, dy):
        blocks = rbuf.at[n, pl.ds(0, len(exchange_group(dy)))]
        remote(blocks, blocks, as_sem.at[n, dy], ar_sem.at[n, dy], CORE).wait_recv()

    def arrange(n, dst, twist):
        for dy in YORDER:
            exchange_wait_recv(n, dy)
            yg = (y - dy + 4) % 4
            lhs = jnp.concatenate(
                [
                    jnp.concatenate(
                        [rbuf[n, yg * 4 + b, :, ch * 128 : ch * 128 + 128] for b in range(4)], axis=1
                    )
                    for ch in range(8)
                ],
                axis=0,
            )
            lanes = pl.ds(pl.multiple_of(yg * 128, 128), 128)
            out = dot(lhs, regroup[...], NN)
            for ch in range(8):
                for cl in range(4):
                    piece = out[ch * 32 : ch * 32 + 32, cl * 128 : cl * 128 + 128]
                    if twist is not None:
                        piece = piece * twist[:, lanes]
                    dst[ch * 4 + cl, :, lanes] = piece.astype(BF)

    def spread(n, left, right, twist):
        @pl.loop(0, 4)
        def _(m):
            out = dot(left, right[pl.ds(m * 8, 8)].reshape(256, 512), NT)
            for part in range(2):
                piece = out[:, part * 128 : part * 128 + 128]
                if twist is not None:
                    piece = piece * twist[...]
                lanes = pl.ds(pl.multiple_of(m * 256 + part * 128, 128), 128)
                sbuf[n, :, :, lanes] = piece.astype(BF).reshape(16, 32, 128)

    def share(n, first, second):
        @pl.loop(0, 4)
        def _(m):
            lanes = pl.ds(pl.multiple_of(m * 128, 128), 128)
            out = dot(first[:, :, lanes].reshape(1024, 128), second[...].reshape(1024, 512), TN)
            out = out.astype(BF)
            for p in range(4):
                gb[n, p % 2, m * 2 + p // 2] = out[p * 32 : p * 32 + 32]

    def core_copy(n):
        return remote(gb.at[n, 1 - co], gc.at[n], gcs_sem.at[n], gcr_sem.at[n], CORE)

    def core_send(n):
        core_copy(n).start()

    def blocks_wait(buf, count, ssem, rsem):
        blocks = buf.at[pl.ds(0, count)]
        return remote(blocks, blocks, ssem, rsem, CORE)

    XY = [(dx, dy) for dx in (2, 1, 3, 0) for dy in (2, 1, 3, 0) if dx or dy]
    Z = [(dh, dl) for dh in (2, 1, 3, 0) for dl in range(2) if dh or dl]

    def xy_wait(n):
        return blocks_wait(xr.at[n], 15, xs_sem.at[n], xr_sem.at[n])

    def z_wait(n):
        return blocks_wait(zr.at[n], 7, zs_sem.at[n], zr_sem.at[n])

    def y_wait(n):
        return blocks_wait(yr.at[n], 3, ys_sem.at[n], yr_sem.at[n])

    def xy_send(n):
        core_copy(n).wait_recv()

        @pl.loop(0, 4)
        def _(m):
            total = gb[n, co, pl.ds(m * 2, 2)].astype(F32) + gc[n, pl.ds(m * 2, 2)].astype(F32)
            total = total.astype(BF).reshape(64, 512)
            for p in range(4):
                xs[n, m * 4 + p] = total[:, p * 128 : p * 128 + 128]

        for dx, dy in XY:
            to = ((x + dx) % 4) * 4 + (y + dy) % 4
            remote(
                xs.at[n, to], xr.at[n, x * 4 + y], xs_sem.at[n], xr_sem.at[n],
                device(dx, 0, 0, dy, 0),
            ).start()
        xr[n, x * 4 + y] = xs[n, x * 4 + y]

    def z_send(n):
        xy_wait(n).wait_recv()
        total = xr[n, 0].astype(F32)
        for p in range(1, 16):
            total = total + xr[n, p].astype(F32)
        zb[n] = total.astype(BF).reshape(2, 32, 128)
        for dh, dl in Z:
            remote(
                zb.at[n, (zl + dl) % 2], zr.at[n, zh * 2 + zl], zs_sem.at[n], zr_sem.at[n],
                device(0, dl, 0, 0, dh),
            ).start()
        zr[n, zh * 2 + zl] = zb[n, zl]

    def y_send(n):
        z_wait(n).wait_recv()
        total = zr[n, 0].astype(F32)
        for p in range(1, 8):
            total = total + zr[n, p].astype(F32)
        yr[n, y] = total * SCALE
        for dy in (2, 1, 3):
            remote(
                yr.at[n, y], yr.at[n, y], ys_sem.at[n], yr_sem.at[n], device(0, 0, 0, dy, 0)
            ).start()

    def finish(n):
        y_wait(n).wait_recv()
        for p in range(4):
            grads[n, :, p * 128 : p * 128 + 128] = yr[n, p]

    def reduce_end(n):
        core_copy(n).wait_send()
        xy_wait(n).wait_send()
        z_wait(n).wait_send()
        y_wait(n).wait_send()

    def outputs(left, f, dims, dst):
        @pl.loop(0, 2)
        def _(n):
            rows = pl.ds(pl.multiple_of(n * 16, 16), 16)
            out = dot(left[:, rows, :].reshape(512, 512), factor(f), dims).astype(BF)
            dst[pl.ds(n * 16, 16)] = dot(perm_out[...], out, NN).astype(BF).reshape(16, 32, 512)

    gather_a(R1, True)
    load_wait(0, kn)
    load_wait(1, vn)
    product(kn, vn, wx)
    shuffle(wx, us)
    gather_b(R1, True)
    for copy in twist_loads:
        copy.wait()
    tw1x[...] = jnp.concatenate([tw1t[...]] * 4, axis=0).T
    tw2x[...] = jnp.concatenate([tw2t[...]] * 4, axis=0).T
    gather_c(R1)
    for f in (L2, L1, R2):
        gather_a(f, False)
    gather_d(R1)
    fact[0] = factor(R1).T
    spread(T1, fact[0], us, tw1x)
    for f in (L2, L1, R2):
        gather_b(f, False)
    exchange_send(T1)

    gather_c(L2)
    load_wait(2, gn)
    load_wait(3, qn)
    product(gn, qn, wx)
    shuffle(wx, gos)
    gather_d(L2)
    spread(DT2, factor(L2), gos, None)
    for f in (L1, R2):
        gather_c(f)
    regroup[...] = grid2(
        (512, 512),
        lambda r, q: (r >> 7 == ((q >> 5) & 3)) & (((r >> 5) & 3) == q >> 7) & ((r & 31) == (q & 31)),
    )
    perm_out[...] = grid2((512, 512), lambda q, r: (r >> 4 == (q & 31)) & ((r & 15) == q >> 5))
    load_wait(4, hn)
    shuffle(hn, hs)
    for f in (L1, R2):
        gather_d(f)
    fact[1] = factor(R2).T
    exchange_send(DT2)

    arrange(T1, t1x, None)

    @pl.loop(0, 4)
    def _(m):
        rows = pl.ds(m * 8, 8)
        out = dot(t1x[rows].reshape(256, 512), factor(L1), NN).reshape(8, 32, 512)
        zs[rows] = out
        wx[rows] = (out * hs[rows].astype(F32)).astype(BF)

    spread(T2, fact[1], wx, tw2x)
    exchange_send(T2)

    arrange(DT2, ds2x, tw2t)

    @pl.loop(0, 2)
    def _(n):
        rows = pl.ds(pl.multiple_of(n * 16, 16), 16)
        out = dot(ds2x[:, rows, :].reshape(512, 512), factor(R2), NT).reshape(32, 16, 512)
        dzx[:, rows, :] = (out * hs[:, rows, :].astype(F32)).astype(BF)
        grad = (out * zs[:, rows, :]).astype(BF).reshape(512, 512)
        hn[pl.ds(n * 16, 16)] = dot(perm_out[...], grad, NN).astype(BF).reshape(16, 32, 512)

    spread(DT1, factor(L1), dzx, None)
    store(2, gh_hbm, hn)
    share(GRO, wx, ds2x)
    core_send(GRO)
    share(GLI, t1x, dzx)
    core_send(GLI)
    xy_send(GRO)
    xy_send(GLI)
    exchange_send(DT1)
    z_send(GRO)
    z_send(GLI)

    arrange(T2, t2x, None)
    share(GLO, t2x, gos)
    core_send(GLO)
    outputs(t2x, L2, NN, qn)
    store(0, o_hbm, qn)
    xy_send(GLO)
    y_send(GRO)
    y_send(GLI)
    z_send(GLO)

    arrange(DT1, ds1x, tw1t)
    share(GRI, us, ds1x)
    core_send(GRI)
    y_send(GLO)
    xy_send(GRI)
    outputs(ds1x, R1, NT, kn)
    store(1, du_hbm, kn)
    for n in (GRO, GLI, GLO):
        finish(n)
    z_send(GRI)
    exchange_end()
    gather_end()
    for n in (GRO, GLI, GLO):
        reduce_end(n)
    y_send(GRI)
    for n, vmem in enumerate((qn, kn, hn)):
        store_wait(n, vmem)
    finish(GRI)
    copy = pltpu.make_async_copy(grads, grads_hbm, own_sem.at[0])
    copy.start()
    reduce_end(GRI)
    copy.wait()


def products(
    o_hbm, du_hbm, gh_hbm, grads_hbm, q_hbm, g_hbm, k_hbm, v_hbm,
    mo_out, gq_out, gk_out, gv_out, gh_out, gri_out, gli_out, gro_out, glo_out,
    value, first, second, through, grads, in_sem, out_sem,
):
    lanes = 16384 // PARTS

    def window(ref, p):
        return ref.at[:, pl.ds(p * lanes, lanes)]

    sources = ((o_hbm, q_hbm, g_hbm), (du_hbm, v_hbm, k_hbm))
    targets = ((mo_out, gq_out), (gk_out, gv_out))
    steps = [(s, p) for s in range(2) for p in range(PARTS)]

    def loads(n):
        s, p = steps[n]
        return [
            pltpu.make_async_copy(window(ref, p), buf.at[n], in_sem.at[n, m])
            for m, (ref, buf) in enumerate(zip(sources[s], (value, first, second)))
        ]

    def stores(n):
        s, p = steps[n]
        return [
            pltpu.make_async_copy(buf.at[n], window(ref, p), out_sem.at[n, m])
            for m, (ref, buf) in enumerate(zip(targets[s], (first, second)))
        ]

    extra = len(steps)
    whole_in = [
        pltpu.make_async_copy(gh_hbm, through, in_sem.at[extra, 0]),
        pltpu.make_async_copy(grads_hbm, grads, in_sem.at[extra, 1]),
    ]
    for n in range(len(steps)):
        for copy in loads(n):
            copy.start()
    for copy in whole_in:
        copy.start()
    for n in range(len(steps)):
        for copy in loads(n):
            copy.wait()
        factor = value[n].astype(F32)
        first[n] = (factor * first[n].astype(F32)).astype(BF)
        second[n] = (factor * second[n].astype(F32)).astype(BF)
        for copy in stores(n):
            copy.start()
    for copy in whole_in:
        copy.wait()
    whole_out = [pltpu.make_async_copy(through, gh_out, out_sem.at[extra, 0])] + [
        pltpu.make_async_copy(grads.at[n], ref, out_sem.at[extra + 1 + n // 2, n % 2])
        for n, ref in ((GRI, gri_out), (GLI, gli_out), (GRO, gro_out), (GLO, glo_out))
    ]
    for copy in whole_out:
        copy.start()
    for n in range(len(steps)):
        for copy in stores(n):
            copy.wait()
    for copy in whole_out:
        copy.wait()


def shards(
    query, key, values, kern, cotangent, rin, lin, rout, lout, twiddle_one, twiddle_two
):
    any_spec = pl.BlockSpec(memory_space=pl.ANY)
    stream = pltpu.VMEM((32, 32, 512), BF)
    dma = pltpu.SemaphoreType.DMA
    wide = jax.ShapeDtypeStruct((32, 16384), BF)
    small = jax.ShapeDtypeStruct((32, 512), F32)
    o, du, gh, grads = pl.pallas_call(
        mixer,
        out_shape=[wide] * 3 + [jax.ShapeDtypeStruct((4, 32, 512), F32)],
        in_specs=[any_spec] * 11,
        out_specs=[any_spec] * 4,
        scratch_shapes=[stream] * 5
        + [stream] * 3
        + [pltpu.VMEM((32, 32, 512), F32)]
        + [pltpu.VMEM((4, 16, 32, 512), BF), pltpu.VMEM((2, 512, 512), BF)]
        + [stream] * 6
        + [pltpu.VMEM((4, 16, 32, 1024), BF)] * 2
        + [pltpu.VMEM((512, 512), BF)] * 3
        + [pltpu.VMEM((512, 128), F32)] * 2
        + [pltpu.VMEM((32, 512), F32)] * 2
        + [
            pltpu.VMEM((4, 2, 8, 32, 512), BF),
            pltpu.VMEM((4, 8, 32, 512), BF),
            pltpu.VMEM((4, 16, 64, 128), BF),
            pltpu.VMEM((4, 16, 64, 128), BF),
            pltpu.VMEM((4, 2, 32, 128), BF),
            pltpu.VMEM((4, 8, 32, 128), BF),
            pltpu.VMEM((4, 4, 32, 128), F32),
            pltpu.VMEM((4, 32, 512), F32),
        ]
        + [
            dma((5,)), dma((6,)), dma((3,)),
            dma((1,)), dma((4, 5)), dma((4, 4)), dma((4, 4)),
            dma((4,)), dma((4,)), dma((4,)), dma((4,)), dma((4,)), dma((4,)),
            dma((4,)), dma((4,)),
        ],
        compiler_params=pltpu.CompilerParams(
            collective_id=0, has_side_effects=True, vmem_limit_bytes=60 << 20
        ),
        cost_estimate=pl.CostEstimate(
            flops=13_000_000_000, bytes_accessed=9 << 20, transcendentals=0
        ),
        name="mixer",
    )(
        query, key, values, kern, cotangent, rin, lin, rout, lout,
        twiddle_one.T, twiddle_two.T,
    )
    part = pltpu.VMEM((2 * PARTS, 32, 16384 // PARTS), BF)
    outs = pl.pallas_call(
        products,
        out_shape=[wide] * 5 + [small] * 4,
        in_specs=[any_spec] * 8,
        out_specs=[any_spec] * 9,
        scratch_shapes=[part] * 3
        + [pltpu.VMEM((32, 16384), BF), pltpu.VMEM((4, 32, 512), F32)]
        + [dma((2 * PARTS + 3, 3))] * 2,
        compiler_params=pltpu.CompilerParams(vmem_limit_bytes=60 << 20),
        cost_estimate=pl.CostEstimate(
            flops=4 << 20, bytes_accessed=13 << 20, transcendentals=0
        ),
        name="products",
    )(o, du, gh, grads, query, cotangent, key, values)
    return tuple(outs)


def solution(mesh):
    wide, rows, cols = P("dp", "seq"), P("dp", None), P(None, "seq")
    return jax.shard_map(
        shards,
        mesh=mesh,
        in_specs=(wide,) * 5 + (rows,) * 4 + (cols,) * 2,
        out_specs=(wide,) * 5 + (rows,) * 4,
        check_vma=False,
    )
```

time: 177 us -> 150 us (0.85)
  local copies, waits for them, and re-layouts: 13.9 us -> 0 us
  Pallas kernels: 161 us -> 149 us
    unnamed x29 -> x0, local copies, waits for them, and re-layouts: 13.9 us -> none
    pallas_call x1 -> x2, Pallas kernels: 161 us -> 149 us  [the longest x1 143 us: shards(): pl.pallas_call(mixer, out_shape=[wide] * 3 + [jax.ShapeDtypeStruct((4, 32...]
where the time goes in v2:
time: 150 us; the launch traced here: 149 us
  Pallas kernels  149 us (99%)
    pallas_call x1, Pallas kernels, shards(): pl.pallas_call(mixer, out_shape=[wide] * 3 + [jax.ShapeDtypeStruct((4, 32...  143 us
    pallas_call x1, Pallas kernels, shards(): pl.pallas_call(products, out_shape=[wide] * 5 + [small] * 4, in_specs=[an...  5.89 us

profile of v2, /device:TPU:2, one launch (start us, length us, event | category | flops | bytes accessed | tf_op | source)
XLA Modules:
  0.0 149.4 jit_solution(18312729228930823843)
XLA Ops:
  0.6 142.9 %mixer.1 = (bf16[32,16384]{1,0:T(8,128)(2,1)}, bf16[32,16384]{1,0:T(8,128)(2,1)}, bf16[32,16384]{1,0:T(8,128)(2,1)}, f32[4,32,512]{2,1,0:T(8,128)}) custom-call(bf16[32,16384]{1,0:T(8,128)(2,1)} %q_hbm.3, bf16[32,16384]{1,0:T(8,128)(2,1)} %k_hbm.3, bf16[32,16384]{1,0:T(8,128)(2,1)} %v_hbm.3, bf16[32,16384]{1,0:T(8,128)(2,1)} %h_hbm.1, ...), custom_call_target="tpu_custom_call" | custom-call | flops 12999999488 | bytes 9437184 | tf_op jit(solution)/shard_map/mixer/pallas_call | solution.py:503
  143.5 5.9 %products.1 = (bf16[32,16384]{1,0:T(8,128)(2,1)}, bf16[32,16384]{1,0:T(8,128)(2,1)}, bf16[32,16384]{1,0:T(8,128)(2,1)}, bf16[32,16384]{1,0:T(8,128)(2,1)}, bf16[...) custom-call(bf16[32,16384]{1,0:T(8,128)(2,1)} %get-tuple-element.13., ...), custom_call_target="tpu_custom_call" | custom-call | flops 4194304 | bytes 13631488 | tf_op jit(solution)/shard_map/products/pallas_call | solution.py:545

commit v3 on v2

--- a/solution.py
+++ b/solution.py
@@ -35,8 +35,10 @@
     us, gos, hs, zs, fac, fact, t1x, wx, ds2x, dzx, t2x, ds1x,
     sbuf, rbuf, perm_in, perm_out, regroup, tw1x, tw2x, tw1t, tw2t,
     gb, gc, xs, xr, zb, zr, yr, grads,
+    ut, xst, xrt, ybt, yrt,
     load_sem, own_sem, out_sem, fs_sem, fr_sem, as_sem, ar_sem,
     gcs_sem, gcr_sem, xs_sem, xr_sem, zs_sem, zr_sem, ys_sem, yr_sem,
+    tile_sem, xrt_sem,
 ):
     dp = lax.axis_index("dp")
     me = lax.axis_index("seq")
@@ -65,8 +67,8 @@
     def load_wait(n, vmem):
         pltpu.make_async_copy(vmem, vmem, load_sem.at[n]).wait()
 
-    def store(n, hbm, vmem):
-        @pl.loop(0, 32)
+    def store(n, hbm, vmem, first=0, last=32):
+        @pl.loop(first, last)
         def _(i):
             pltpu.make_async_copy(
                 vmem.at[i], hbm.at[:, pl.ds(pl.multiple_of(i * 512, 512), 512)], out_sem.at[n]
@@ -80,6 +82,7 @@
         + [(dx, 0, 0, dy, 0) for dx in range(1, 4) for dy in range(4)]
         + [(0, 1, 0, 0, dh) for dh in range(4)]
         + [(dx, 1, 0, 0, 0) for dx in range(1, 4)]
+        + [(dx, 0, 1, 0, 0) for dx in range(1, 4)]
         + [(0, 0, 1, 0, 0)]
     )
     barrier = pltpu.get_barrier_semaphore()
@@ -198,8 +201,8 @@
         blocks = rbuf.at[n, pl.ds(0, len(exchange_group(dy)))]
         remote(blocks, blocks, as_sem.at[n, dy], ar_sem.at[n, dy], CORE).wait_recv()
 
-    def arrange(n, dst, twist):
-        for dy in YORDER:
+    def arrange(n, dst, twist, group=YORDER):
+        for dy in group:
             exchange_wait_recv(n, dy)
             yg = (y - dy + 4) % 4
             lhs = jnp.concatenate(
@@ -285,6 +288,9 @@
         total = xr[n, 0].astype(F32)
         for p in range(1, 16):
             total = total + xr[n, p].astype(F32)
+        z_spread(n, total)
+
+    def z_spread(n, total):
         zb[n] = total.astype(BF).reshape(2, 32, 128)
         for dh, dl in Z:
             remote(
@@ -309,14 +315,57 @@
         for p in range(4):
             grads[n, :, p * 128 : p * 128 + 128] = yr[n, p]
 
+    def tile_share(dy):
+        lanes = pl.ds(pl.multiple_of(((y - dy + 4) % 4) * 128, 128), 128)
+        out = dot(ut[...], ds1x[:, :, lanes].reshape(1024, 128), NN).astype(BF)
+        for m in range(16):
+            half = (m // 2) % 2 * 32
+            xst[dy, m // 4 * 2 + m % 2, half : half + 32] = out[m * 32 : m * 32 + 32]
+        for dx, dc in XC:
+            to = ((x + dx) % 4) * 2 + (co + dc) % 2
+            remote(
+                xst.at[dy, to], xrt.at[dy, x * 2 + co], tile_sem.at[1], xrt_sem.at[dy],
+                device(dx, 0, dc, 0, 0),
+            ).start()
+        xrt[dy, x * 2 + co] = xst[dy, x * 2 + co]
+
+    XC = [(dx, dc) for dx in (2, 1, 3, 0) for dc in (1, 0) if dx or dc]
+
+    def tile_x_wait(dy):
+        blocks_wait(xrt.at[dy], 7, tile_sem.at[1], xrt_sem.at[dy]).wait_recv()
+        total = xrt[dy, 0].astype(F32)
+        for p in range(1, 8):
+            total = total + xrt[dy, p].astype(F32)
+        return total
+
+    def tile_y(dy):
+        ybt[dy] = tile_x_wait(dy).astype(BF)
+        remote(
+            ybt.at[dy], yrt.at[dy], tile_sem.at[2], tile_sem.at[3], device(0, 0, 0, 4 - dy, 0)
+        ).start()
+
+    def tile_z():
+        total = tile_x_wait(0)
+        blocks_wait(yrt, 3, tile_sem.at[2], tile_sem.at[3]).wait_recv()
+        for dy in (1, 2, 3):
+            total = total + yrt[dy].astype(F32)
+        z_spread(GRI, total)
+
+    def tile_end():
+        sent = xst.at[:, pl.ds(0, 7)]
+        remote(sent, sent, tile_sem.at[1], xrt_sem.at[0], CORE).wait_send()
+        blocks_wait(ybt, 3, tile_sem.at[2], tile_sem.at[3]).wait_send()
+        z_wait(GRI).wait_send()
+        y_wait(GRI).wait_send()
+
     def reduce_end(n):
         core_copy(n).wait_send()
         xy_wait(n).wait_send()
         z_wait(n).wait_send()
         y_wait(n).wait_send()
 
-    def outputs(left, f, dims, dst):
-        @pl.loop(0, 2)
+    def outputs(left, f, dims, dst, first=0, last=2):
+        @pl.loop(first, last)
         def _(n):
             rows = pl.ds(pl.multiple_of(n * 16, 16), 16)
             out = dot(left[:, rows, :].reshape(512, 512), factor(f), dims).astype(BF)
@@ -347,10 +396,11 @@
     load_wait(3, qn)
     product(gn, qn, wx)
     shuffle(wx, gos)
+    gather_c(L1)
+    gather_c(R2)
     gather_d(L2)
     spread(DT2, factor(L2), gos, None)
-    for f in (L1, R2):
-        gather_c(f)
+    exchange_send(DT2)
     regroup[...] = grid2(
         (512, 512),
         lambda r, q: (r >> 7 == ((q >> 5) & 3)) & (((r >> 5) & 3) == q >> 7) & ((r & 31) == (q & 31)),
@@ -358,12 +408,9 @@
     perm_out[...] = grid2((512, 512), lambda q, r: (r >> 4 == (q & 31)) & ((r & 15) == q >> 5))
     load_wait(4, hn)
     shuffle(hn, hs)
-    for f in (L1, R2):
-        gather_d(f)
-    fact[1] = factor(R2).T
-    exchange_send(DT2)
 
     arrange(T1, t1x, None)
+    gather_d(L1)
 
     @pl.loop(0, 4)
     def _(m):
@@ -372,6 +419,8 @@
         zs[rows] = out
         wx[rows] = (out * hs[rows].astype(F32)).astype(BF)
 
+    gather_d(R2)
+    fact[1] = factor(R2).T
     spread(T2, fact[1], wx, tw2x)
     exchange_send(T2)
 
@@ -400,34 +449,44 @@
     arrange(T2, t2x, None)
     share(GLO, t2x, gos)
     core_send(GLO)
+    ut[...] = us[...].reshape(1024, 512).T
     outputs(t2x, L2, NN, qn)
     store(0, o_hbm, qn)
-    xy_send(GLO)
     y_send(GRO)
     y_send(GLI)
+
+    arrange(DT1, ds1x, tw1t, YORDER[:1])
+    tile_share(1)
+    arrange(DT1, ds1x, tw1t, YORDER[1:2])
+    tile_share(2)
+    xy_send(GLO)
+    arrange(DT1, ds1x, tw1t, YORDER[2:3])
+    tile_share(3)
+    tile_y(1)
+    arrange(DT1, ds1x, tw1t, YORDER[3:])
+    tile_share(0)
+    tile_y(2)
+    tile_y(3)
     z_send(GLO)
-
-    arrange(DT1, ds1x, tw1t)
-    share(GRI, us, ds1x)
-    core_send(GRI)
+    outputs(ds1x, R1, NT, kn, 0, 1)
+    tile_z()
     y_send(GLO)
-    xy_send(GRI)
-    outputs(ds1x, R1, NT, kn)
-    store(1, du_hbm, kn)
+    store(1, du_hbm, kn, 0, 16)
+    outputs(ds1x, R1, NT, kn, 1, 2)
+    store(1, du_hbm, kn, 16, 32)
+    y_send(GRI)
     for n in (GRO, GLI, GLO):
         finish(n)
-    z_send(GRI)
     exchange_end()
     gather_end()
     for n in (GRO, GLI, GLO):
         reduce_end(n)
-    y_send(GRI)
     for n, vmem in enumerate((qn, kn, hn)):
         store_wait(n, vmem)
     finish(GRI)
     copy = pltpu.make_async_copy(grads, grads_hbm, own_sem.at[0])
     copy.start()
-    reduce_end(GRI)
+    tile_end()
     copy.wait()
 
 
@@ -523,12 +582,17 @@
             pltpu.VMEM((4, 8, 32, 128), BF),
             pltpu.VMEM((4, 4, 32, 128), F32),
             pltpu.VMEM((4, 32, 512), F32),
+            pltpu.VMEM((512, 1024), BF),
+            pltpu.VMEM((4, 8, 64, 128), BF),
+            pltpu.VMEM((4, 8, 64, 128), BF),
+            pltpu.VMEM((4, 64, 128), BF),
+            pltpu.VMEM((4, 64, 128), BF),
         ]
         + [
             dma((5,)), dma((6,)), dma((3,)),
             dma((1,)), dma((4, 5)), dma((4, 4)), dma((4, 4)),
             dma((4,)), dma((4,)), dma((4,)), dma((4,)), dma((4,)), dma((4,)),
-            dma((4,)), dma((4,)),
+            dma((4,)), dma((4,)), dma((4,)), dma((4,)),
         ],
         compiler_params=pltpu.CompilerParams(
             collective_id=0, has_side_effects=True, vmem_limit_bytes=60 << 20

time: 150 us -> 146 us (0.973)
  Pallas kernels: 149 us -> 144 us
    pallas_call x1, Pallas kernels: 143 us -> 138 us  [shards(): pl.pallas_call(mixer, out_shape=[wide] * 3 + [jax.ShapeDtypeStruct((4, 32...]
where the time goes in v3:
time: 146 us; the launch traced here: 144 us
  Pallas kernels  144 us (99%)
    pallas_call x1, Pallas kernels, shards(): pl.pallas_call(mixer, out_shape=[wide] * 3 + [jax.ShapeDtypeStruct((4, 32...  138 us
    pallas_call x1, Pallas kernels, shards(): pl.pallas_call(products, out_shape=[wide] * 5 + [small] * 4, in_specs=[an...  5.89 us

profile of v3, /device:TPU:2, one launch (start us, length us, event | category | flops | bytes accessed | tf_op | source)
XLA Modules:
  0.0 144.3 jit_solution(8455566860444055686)
XLA Ops:
  0.6 137.8 %mixer.1 = (bf16[32,16384]{1,0:T(8,128)(2,1)}, bf16[32,16384]{1,0:T(8,128)(2,1)}, bf16[32,16384]{1,0:T(8,128)(2,1)}, f32[4,32,512]{2,1,0:T(8,128)}) custom-call(bf16[32,16384]{1,0:T(8,128)(2,1)} %q_hbm.3, bf16[32,16384]{1,0:T(8,128)(2,1)} %k_hbm.3, bf16[32,16384]{1,0:T(8,128)(2,1)} %v_hbm.3, bf16[32,16384]{1,0:T(8,128)(2,1)} %h_hbm.1, ...), custom_call_target="tpu_custom_call" | custom-call | flops 12999999488 | bytes 9437184 | tf_op jit(solution)/shard_map/mixer/pallas_call | solution.py:562
  138.5 5.9 %products.1 = (bf16[32,16384]{1,0:T(8,128)(2,1)}, bf16[32,16384]{1,0:T(8,128)(2,1)}, bf16[32,16384]{1,0:T(8,128)(2,1)}, bf16[32,16384]{1,0:T(8,128)(2,1)}, bf16[...) custom-call(bf16[32,16384]{1,0:T(8,128)(2,1)} %get-tuple-element.13., ...), custom_call_target="tpu_custom_call" | custom-call | flops 4194304 | bytes 13631488 | tf_op jit(solution)/shard_map/products/pallas_call | solution.py:609
